TPU v7x, 32 devices: a whole 2x2x4 slice. The times are simulated.
32 devices in a mesh: parts: 2 (over y), group: 4 (over z), tensor: 4 (over x, core).
Axes of the slice: x: 2, y: 2, z: 4, core: 2. Of those that a mesh axis runs over, the one named last changes fastest.
Arguments:
- queries: bfloat16 [512, 8192], P(('parts', 'group'), 'tensor'), parts along dimension 0, may hold values from -36 to 36
- keys: bfloat16 [512, 1024], P(('parts', 'group'), 'tensor'), parts along dimension 0, may hold values from -64 to 64
- values: bfloat16 [512, 1024], P(('parts', 'group'), 'tensor'), parts along dimension 0, may hold values from -6 to 6
- prefix_keys: bfloat16 [2048, 1024], P(('parts', 'group'), 'tensor'), parts along dimension 0, may hold values from -6 to 6
- prefix_values: bfloat16 [2048, 1024], P(('parts', 'group'), 'tensor'), parts along dimension 0, may hold values from -6 to 6
- spread: int32 [8], P('parts'), parts along dimension 0, may hold values from 0 to 3, as said below
- turn: int32 [8], P('parts'), parts along dimension 0, may hold values from 0 to 7
- new_blocks: int32 [8, 4], P('parts'), parts along dimension 0, may hold values from 1 to 2, as said below
- prefix_len: int32 [8, 4], P('parts'), parts along dimension 0, may hold values from 1 to 64, as said below
- owner: int32 [8, 4], P('parts'), parts along dimension 0, may hold values from 0 to 3, as said below
- page_start: int32 [8, 4], P('parts'), parts along dimension 0, may hold values from 0 to 6, as said below
Outputs:
- attention: bfloat16 [512, 8192], P(('parts', 'group'), 'tensor'), parts along dimension 0
- cache: bfloat16 [64, 2, 8, 1024], P(('parts', 'group'), None, 'tensor'), parts along dimension 0
There are 2 independent parts, one for each index of `parts`. A program takes and returns all parts, laid end to end along the dimension named above; each array names one. Nothing has to cross between parts.
Inputs may be any that keep to these rules, and one draw needn't show every extreme that they name: `spread`: A permutation of the numbers below 4. `new_blocks`: in every group one prompt has exactly 2 new blocks. `prefix_len`: in every group one prompt has exactly 64 cached tokens. `owner`: the prompts of one prefill group have different owners, and every decode group owns exactly one prompt of each index p. `page_start`: A multiple of 2; the prompts owned by one decode group start at different pages.
All inputs are finite; a program needn't handle non-finite values.
Results may differ from a plain program's by a relative error of at most 0.012.
The roundings to bfloat16 on the way count: a program that leaves them out, or rounds other values in their place, can miss the bound.
Values may be sent and summed in bfloat16 or wider, within the bound.
No kernel may reach another device: no remote copies, remote signals or barrier semaphores. Data moves between devices by JAX's collectives and lax.ppermute only.
A program may use at most 64 MiB of HBM per device.

v0:
```python
import functools
import math

import jax
import jax.numpy as jnp
import numpy as np
from jax import lax
from jax.experimental import pallas as pl
from jax.experimental.pallas import tpu as pltpu
from jax.sharding import PartitionSpec as P

HEAD = 128
BLOCK = 8
MAXP = 2
CTXP = 64

VMEM_LIMIT = 24 * 1024 * 1024

SMEM = pl.BlockSpec(memory_space=pltpu.SMEM)
VMEM = pl.BlockSpec(memory_space=pltpu.VMEM)
PROMPT, OFFSET, LIVE, CACHED, SOURCE, COLUMN = range(6)
ANY = pl.BlockSpec(memory_space=pl.ANY)
HBM = pl.BlockSpec(memory_space=pltpu.HBM)


def rope_table():
    count = CTXP + MAXP * BLOCK
    half = HEAD // 2
    frequency = np.exp(np.arange(half) * (-2.0 * math.log(500000.0) / HEAD))
    angles = np.arange(count)[:, None] * frequency[None, :]
    cosine, sine = np.cos(angles), np.sin(angles)
    return (
        np.concatenate([cosine, cosine], axis=1).astype(np.float32),
        np.concatenate([-sine, sine], axis=1).astype(np.float32),
    )


def loop(count, body, unrolled=16):
    if count <= unrolled:
        for index in range(count):
            body(index)
    else:
        lax.fori_loop(0, count, lambda index, carry: (body(index), carry)[1], 0)


def turned(head_block, cosine, sine):
    return head_block * cosine + pltpu.roll(head_block, HEAD // 2, 1) * sine


def dispatch_kernel(groups, spread_in, turn_in, queries_in, keys_in, values_in, *rest):
    outs, (spread, turn, queries, keys, values, sem) = rest[:groups], rest[groups:]
    own = lax.axis_index("group")
    slots, _, width_q = queries.shape
    width_k = keys.shape[2]
    capacity = slots // groups
    copies = [
        pltpu.make_async_copy(source, target, sem.at[n])
        for n, (source, target) in enumerate(
            (
                (spread_in, spread),
                (turn_in, turn),
                (queries_in, queries),
                (keys_in, keys),
                (values_in, values),
            )
        )
    ]
    for copy in copies:
        copy.start()
    for copy in copies[:2]:
        copy.wait()
    sources = []
    for distance in range(groups):
        first_slot = column_of(spread, groups, distance) + turn[own]
        sources.append([lax.rem(first_slot + groups * step, slots) for step in range(capacity)])
    for copy in copies[2:]:
        copy.wait()
    for distance in range(groups):
        for step in range(capacity):
            source = sources[distance][step]
            out = outs[distance]
            out[step, :, :width_q] = queries[source]
            out[step, :, width_q : width_q + width_k] = keys[source]
            out[step, :, width_q + width_k :] = values[source]


def column_of(spread, groups, distance):
    wanted = (groups - distance) % groups
    if groups <= 8:
        return sum(jnp.where(spread[c] == wanted, c, 0) for c in range(groups))
    return lax.fori_loop(
        0, groups, lambda c, found: jnp.where(spread[c] == wanted, c, found), jnp.int32(0)
    )


def make_plan(groups, own, spread, new_blocks, prefix_len, owner, page_start, plan):
    prompts = new_blocks.shape[1]
    slots = prompts * MAXP

    def clear(j):
        plan[PROMPT, j] = 0
        plan[OFFSET, j] = 0
        plan[LIVE, j] = 0
        plan[CACHED, j] = 0

    loop(slots, clear)

    def one(p, start):
        blocks = new_blocks[own, p]
        cached = prefix_len[own, p]
        for step in range(MAXP):
            at = jnp.where(step < blocks, start + step, slots)
            plan[PROMPT, at] = p
            plan[OFFSET, at] = cached + step * BLOCK
            plan[LIVE, at] = 1 + step
            plan[CACHED, at] = cached
        return start + blocks

    start = jnp.int32(0)
    if prompts <= 8:
        for p in range(prompts):
            start = one(p, start)
    else:
        lax.fori_loop(0, prompts, one, start)

    def of_group(g):
        def one(p, start):
            blocks = new_blocks[g, p]
            mine = owner[g, p] == own
            for step in range(MAXP):
                root = lax.rem(g + spread[lax.rem(start + step, groups)], groups)
                at = jnp.where(mine, page_start[g, p] + step, slots)
                plan[SOURCE, at] = jnp.where(step < blocks, root * groups + g, -1)
            return start + blocks

        start = jnp.int32(0)
        if prompts <= 8:
            for p in range(prompts):
                start = one(p, start)
        else:
            lax.fori_loop(0, prompts, one, start)

    loop(groups, of_group)
    for distance in range(groups):
        plan[COLUMN, distance] = column_of(spread, groups, distance)


def pages_kernel(
    groups, tensors, spread, turn, new_blocks, prefix_len, owner, page_start, keys, values, cosine, sine,
    _, out, plan, rows, dest_group, dest_owner,
):
    own = lax.axis_index("group")
    slots, _, width_k = keys.shape
    capacity = slots // groups
    prompts = new_blocks.shape[1]
    tokens = BLOCK // tensors

    def column(c):
        target = lax.rem(own - spread[c] + groups, groups)
        for step in range(capacity):
            j = c + groups * step
            source = lax.rem(j + turn[own], slots)

            def find(p, carry):
                start, place, holder = carry
                blocks = new_blocks[target, p]
                inside = (j >= start) & (j < start + blocks)
                place = jnp.where(inside, prefix_len[target, p] + (j - start) * BLOCK, place)
                holder = jnp.where(inside, owner[target, p], holder)
                return start + blocks, place, holder

            carry = (jnp.int32(0), jnp.int32(0), jnp.int32(-1))
            if prompts <= 8:
                for p in range(prompts):
                    carry = find(p, carry)
            else:
                carry = lax.fori_loop(0, prompts, find, carry)
            _, place, holder = carry
            dest_group[source] = target
            dest_owner[source] = holder
            cos = cosine[pl.ds(place, BLOCK), :]
            sin = sine[pl.ds(place, BLOCK), :]
            block = keys[source].astype(jnp.float32)
            at = pl.multiple_of(source * BLOCK, BLOCK)
            rows[pl.ds(at, BLOCK), :] = jnp.concatenate(
                [
                    turned(block[:, h * HEAD : (h + 1) * HEAD], cos, sin)
                    for h in range(width_k // HEAD)
                ],
                axis=1,
            )
            at = pl.multiple_of((slots + source) * BLOCK, BLOCK)
            rows[pl.ds(at, BLOCK), :] = values[source].astype(jnp.float32)

    loop(groups, column)
    body = rows[...].astype(jnp.bfloat16)
    part = 2 * tokens
    shape = (tensors * groups * part, 2 * slots * BLOCK)
    row = lax.broadcasted_iota(jnp.int32, shape, 0)
    col = lax.broadcasted_iota(jnp.int32, shape, 1)
    row_tensor = row // (groups * part)
    row_group = (row // part) % groups
    same = ((row // tokens) % 2 == col // (slots * BLOCK)) & (
        row_tensor * tokens + row % tokens == col % BLOCK
    )
    code = jnp.where(same, row_group * slots + (col // BLOCK) % slots, -1)

    def send(d):
        def mark(b, total):
            wanted = jnp.where(dest_owner[b] == d, dest_group[b] * slots + b, -2)
            return total | (code == wanted)

        if slots <= 8:
            total = code == -2
            for b in range(slots):
                total = mark(b, total)
            pick = total.astype(jnp.float32)
        else:
            pick = lax.fori_loop(
                0,
                slots,
                lambda b, total: jnp.where(
                    code == jnp.where(dest_owner[b] == d, dest_group[b] * slots + b, -2), 1.0, total
                ),
                jnp.zeros(shape, jnp.float32),
            )
        moved = jnp.dot(pick.astype(jnp.bfloat16), body, preferred_element_type=jnp.float32)
        out[pl.ds(d * tensors, tensors)] = moved.astype(jnp.bfloat16).reshape(
            tensors, groups * part, width_k
        )

    loop(groups, send)
    make_plan(groups, own, spread, new_blocks, prefix_len, owner, page_start, plan)


def attention_kernel(groups, heads_q, heads_k, plan, prefix_keys, prefix_values, cosine, sine, *rest):
    arrived, (out, new_keys, new_values) = rest[:groups], rest[groups:]
    slots = out.shape[0]
    capacity = slots // groups
    ratio = heads_q // heads_k
    width_q = heads_q * HEAD
    width_k = heads_k * HEAD
    scale = math.log2(math.e) / math.sqrt(HEAD)
    span = CTXP + 2 * BLOCK
    lane = lax.broadcasted_iota(jnp.int32, (BLOCK, span), 1)
    token = lax.broadcasted_iota(jnp.int32, (BLOCK, span), 0)
    fresh = (lane >= CTXP + BLOCK) & (lane - (CTXP + BLOCK) <= token)
    before = (lane >= CTXP) & (lane < CTXP + BLOCK)

    blocks = []
    for distance in range(groups):
        first_slot = plan[COLUMN, distance]
        for step in range(capacity):
            j = first_slot + groups * step
            here = arrived[distance].at[step]
            cos = cosine[pl.ds(plan[OFFSET, j], BLOCK), :]
            sin = sine[pl.ds(plan[OFFSET, j], BLOCK), :]
            new_keys[j] = jnp.concatenate(
                [
                    turned(here[:, first : first + HEAD].astype(jnp.float32), cos, sin)
                    for first in range(width_q, width_q + width_k, HEAD)
                ],
                axis=1,
            )
            new_values[j] = here[:, width_q + width_k :].astype(jnp.float32)
            blocks.append((j, here, cos, sin))

    for at in range(0, len(blocks), 8):
        some = blocks[at : at + 8]
        for h in range(heads_k):
            part = slice(h * HEAD, (h + 1) * HEAD)
            scores = []
            for j, here, cos, sin in some:
                prev = jnp.maximum(j - 1, 0)
                region = pl.ds(pl.multiple_of(plan[PROMPT, j] * CTXP, CTXP), CTXP)
                mask = fresh | (lane < plan[CACHED, j]) & (lane < CTXP) | before & (plan[LIVE, j] == 2)
                new_key = jnp.concatenate([new_keys[prev, :, part], new_keys[j, :, part]], axis=0)
                key = jnp.concatenate([prefix_keys[region, part], new_key.astype(jnp.bfloat16)], axis=0)
                query = jnp.concatenate(
                    [
                        turned(here[:, n * HEAD : (n + 1) * HEAD].astype(jnp.float32), cos, sin)
                        for n in range(h * ratio, (h + 1) * ratio)
                    ],
                    axis=0,
                ).astype(jnp.bfloat16)
                score = lax.dot_general(
                    query, key, (((1,), (1,)), ((), ())), preferred_element_type=jnp.float32
                )
                scores.append(jnp.where(mask[None], score.reshape(ratio, BLOCK, span), -1e30))
            score = jnp.concatenate(scores, axis=0)
            top = jnp.max(score, axis=2, keepdims=True)
            powers = jnp.exp2((score - top) * scale)
            weights = powers * (1.0 / jnp.sum(powers, axis=2, keepdims=True))
            weights = weights.reshape(len(some), ratio * BLOCK, span).astype(jnp.bfloat16)
            for place, (j, here, cos, sin) in enumerate(some):
                prev = jnp.maximum(j - 1, 0)
                region = pl.ds(pl.multiple_of(plan[PROMPT, j] * CTXP, CTXP), CTXP)
                new_value = jnp.concatenate([new_values[prev, :, part], new_values[j, :, part]], axis=0)
                value = jnp.concatenate([prefix_values[region, part], new_value.astype(jnp.bfloat16)], axis=0)
                mixed = jnp.dot(weights[place], value, preferred_element_type=jnp.float32)
                mixed = jnp.where(plan[LIVE, j] > 0, mixed, 0.0)
                for n in range(ratio):
                    first = (h * ratio + n) * HEAD
                    out[j, :, first : first + HEAD] = mixed[n * BLOCK : (n + 1) * BLOCK].astype(
                        jnp.bfloat16
                    )


def cache_kernel(groups, tensors, plan, arrived, out):
    tokens = BLOCK // tensors
    part = 2 * tokens
    pages = out.shape[0] // 2
    shape = (pages * part, groups * groups * part)
    row = lax.broadcasted_iota(jnp.int32, shape, 0)
    col = lax.broadcasted_iota(jnp.int32, shape, 1)
    limit = groups * groups
    code = jnp.where(row % part == col % part, (row // part) * limit + col // part, -1)

    def mark(page, total):
        wanted = jnp.where(plan[SOURCE, page] >= 0, page * limit + plan[SOURCE, page], -2)
        return jnp.where(code == wanted, 1.0, total)

    pick = jnp.zeros(shape, jnp.float32)
    if pages <= 8:
        for page in range(pages):
            pick = mark(page, pick)
    else:
        pick = lax.fori_loop(0, pages, mark, pick)
    pick = pick.astype(jnp.bfloat16)
    width_k = arrived.shape[3]
    for t in range(tensors):
        body = arrived[:, t].reshape(groups * groups * part, width_k)
        moved = jnp.dot(pick, body, preferred_element_type=jnp.float32)
        out[:, :, t * width_k : (t + 1) * width_k] = moved.reshape(
            pages * 2, tokens, width_k
        ).astype(jnp.bfloat16)


def per_device(
    queries,
    keys,
    values,
    prefix_keys,
    prefix_values,
    spread,
    turn,
    new_blocks,
    prefix_len,
    owner,
    page_start,
):
    groups = lax.axis_size("group")
    tensors = lax.axis_size("tensor")
    width_q = queries.shape[1]
    width_k = keys.shape[1]
    heads_q = width_q // HEAD
    heads_k = width_k // HEAD
    slots = queries.shape[0] // BLOCK
    capacity = slots // groups
    prompts = new_blocks.shape[1]
    tokens = BLOCK // tensors
    pages = prompts * MAXP
    cosine, sine = (jnp.asarray(table) for table in rope_table())
    params = pltpu.CompilerParams(vmem_limit_bytes=VMEM_LIMIT)
    blocks_q = queries.reshape(slots, BLOCK, width_q)
    blocks_k = keys.reshape(slots, BLOCK, width_k)
    blocks_v = values.reshape(slots, BLOCK, width_k)

    chunk = jax.ShapeDtypeStruct((capacity, BLOCK, width_q + 2 * width_k), jnp.bfloat16)
    sent = pl.pallas_call(
        functools.partial(dispatch_kernel, groups),
        out_shape=[chunk] * groups,
        in_specs=[HBM] * 5,
        out_specs=[VMEM] * groups,
        scratch_shapes=[pltpu.SMEM((groups,), jnp.int32)] * 2
        + [pltpu.VMEM(blocks.shape, jnp.bfloat16) for blocks in (blocks_q, blocks_k, blocks_v)]
        + [pltpu.SemaphoreType.DMA((5,))],
        compiler_params=params,
        cost_estimate=pl.CostEstimate(flops=10**6, bytes_accessed=5 * 10**6, transcendentals=0),
        name="dispatch",
    )(
        *(
            pltpu.with_memory_space_constraint(operand, pltpu.HBM)
            for operand in (spread, turn, blocks_q, blocks_k, blocks_v)
        )
    )
    arrived = [sent[0]] + [
        lax.ppermute(sent[d], "group", [(g, (g + d) % groups) for g in range(groups)])
        for d in range(1, groups)
    ]

    finished, plan = pl.pallas_call(
        functools.partial(pages_kernel, groups, tensors),
        out_shape=[
            jax.ShapeDtypeStruct((groups * tensors, groups * 2 * tokens, width_k), jnp.bfloat16),
            jax.ShapeDtypeStruct((6, max(slots, groups) + 1), jnp.int32),
        ],
        in_specs=[SMEM] * 6 + [VMEM] * 4 + [ANY],
        out_specs=[VMEM, SMEM],
        compiler_params=params,
        scratch_shapes=[
            pltpu.VMEM((2 * slots * BLOCK, width_k), jnp.float32),
            pltpu.SMEM((slots,), jnp.int32),
            pltpu.SMEM((slots,), jnp.int32),
        ],
        cost_estimate=pl.CostEstimate(flops=10**7, bytes_accessed=6 * 10**6, transcendentals=0),
        name="finish_pages",
    )(
        spread, turn, new_blocks, prefix_len, owner, page_start, blocks_k, blocks_v, cosine, sine, sent[0]
    )
    handed = lax.all_to_all(finished, ("group", "tensor"), split_axis=0, concat_axis=0, tiled=True)

    attention = pl.pallas_call(
        functools.partial(attention_kernel, groups, heads_q, heads_k),
        out_shape=jax.ShapeDtypeStruct((slots, BLOCK, width_q), jnp.bfloat16),
        in_specs=[SMEM] + [VMEM] * (4 + groups),
        out_specs=VMEM,
        scratch_shapes=[pltpu.VMEM((slots, BLOCK, width_k), jnp.float32)] * 2,
        compiler_params=params,
        cost_estimate=pl.CostEstimate(flops=10**8, bytes_accessed=15 * 10**6, transcendentals=0),
        name="attention",
    )(plan, prefix_keys, prefix_values, cosine, sine, *arrived)

    cache = pl.pallas_call(
        functools.partial(cache_kernel, groups, tensors),
        out_shape=jax.ShapeDtypeStruct((pages * 2, tokens, tensors * width_k), jnp.bfloat16),
        in_specs=[SMEM, VMEM],
        out_specs=VMEM,
        compiler_params=params,
        cost_estimate=pl.CostEstimate(flops=10**6, bytes_accessed=5 * 10**6, transcendentals=0),
        name="place_pages",
    )(plan, handed.reshape(groups, tensors, groups * 2 * tokens, width_k))
    return (
        attention.reshape(slots * BLOCK, width_q),
        cache.reshape(pages, 2, tokens, tensors * width_k),
    )


def solution(mesh):
    return jax.shard_map(
        per_device,
        mesh=mesh,
        in_specs=(
            P(("parts", "group"), "tensor"),
            P(("parts", "group"), "tensor"),
            P(("parts", "group"), "tensor"),
            P(("parts", "group"), "tensor"),
            P(("parts", "group"), "tensor"),
            P("parts"),
            P("parts"),
            P("parts", None),
            P("parts", None),
            P("parts", None),
            P("parts", None),
        ),
        out_specs=(P(("parts", "group"), "tensor"), P(("parts", "group"), None, "tensor", None)),
        check_vma=False,
    )
```

profile of v0, /device:TPU:0, one launch (start us, length us, event | category | flops | bytes accessed | tf_op | source)
XLA Modules:
  0.0 28.2 jit_solution(13679779736742583764)
XLA Ops:
  0.6 0.0 copy-start
  0.6 0.0 copy-start.1
  0.7 0.0 copy-start.4
  0.7 0.0 copy-start.5
  0.7 0.0 copy-start.6
  0.7 0.0 copy-start.7
  0.7 1.1 %dispatch.1 = (bf16[2,8,2560]{2,1,0:T(8,128)(2,1)S(1)}, bf16[2,8,2560]{2,1,0:T(8,128)(2,1)S(1)}, bf16[2,8,2560]{2,1,0:T(8,128)(2,1)S(1)}, bf16[2,8,2560]{2,1,0:T(8,128)(2,1)S(1)}) custom-call(s32[4]{0:T(128)} %spread.1, s32[4]{0:T(128)} %turn.1, bf16[8,8,2048]{2,1,0:T(8,128)(2,1)} %bitcast.12, bf16[8,8,256]{2,1,0:T(8,128)(2,1)} %bitcast.7, ...), custom_call_target="tpu_custom_call" | custom-call | flops 1000000 | bytes 5000000 | tf_op jit(solution)/shard_map/dispatch/pallas_call | solution.py:370
  1.8 0.0 copy-start.10
  1.8 0.0 copy-start.11
  1.9 0.6 %copy-done.10 = s32[4]{0:T(128)S(1)} copy-done((s32[4]{0:T(128)S(1)}, s32[4]{0:T(128)}, u32[]{:S(2)}) %copy-start.10) | copy-done | bytes 40
  2.5 0.0 copy-done.11
  2.5 2.0 %finish_pages.1 = (bf16[16,16,256]{2,1,0:T(8,128)(2,1)}, s32[6,9]{1,0:T(8,128)S(1)}) custom-call(s32[4]{0:T(128)S(1)} %copy-done.10, s32[4]{0:T(128)S(1)} %copy-done.11, s32[4,4]{1,0:T(4,128)S(1)} %copy-done.6, s32[4,4]{1,0:T(4,128)S(1)} %copy-done.7, s32[4,4]{1,0:T(4,128)S(1)} %copy-done.8, s32[4,4]{1,0:T(4,128)S(1)} %copy-done.9, ...), custom_call_target="tpu_custom_call" | custom-call | flops 10000000 | bytes 6000000 | tf_op jit(solution)/shard_map/finish_pages/pallas_call | solution.py:392
  4.4 0.0 copy-start.2
  4.5 0.0 copy-start.3
  4.5 7.5 %all-to-all-start = ((bf16[16,16,256]{2,1,0:T(8,128)(2,1)}), bf16[16,16,256]{2,1,0:T(8,128)(2,1)S(1)}, u32[]{:S(2)}, u32[]{:S(2)}) async-start(bf16[16,16,256]{2,1,0:T(8,128)(2,1)} %get-tuple-element.13), calls=%async_computation | async-start | bytes 262144 | tf_op jit(solution)/shard_map/all_to_all | solution.py:411
  12.0 1.9 %collective-permute-start = (bf16[2,8,2560]{2,1,0:T(8,128)(2,1)S(1)}, bf16[2,8,2560]{2,1,0:T(8,128)(2,1)S(1)}, u32[]{:S(2)}, u32[]{:S(2)}) collective-permute-start(bf16[2,8,2560]{2,1,0:T(8,128)(2,1)S(1)} %get-tuple-element.10), channel_id=1, source_target_pairs={{0,4},{4,8},{8,12},{12,0},{1,5},{5,9},{9,13},{13,1},{2,6},{6,10},{... | collective-permute-start | bytes 245768 | tf_op jit(solution)/shard_map/ppermute | solution.py:388
  13.9 2.4 %collective-permute-start.1 = (bf16[2,8,2560]{2,1,0:T(8,128)(2,1)S(1)}, bf16[2,8,2560]{2,1,0:T(8,128)(2,1)S(1)}, u32[]{:S(2)}, u32[]{:S(2)}) collective-permute-start(bf16[2,8,2560]{2,1,0:T(8,128)(2,1)S(1)} %get-tuple-element.11), channel_id=1, source_target_pairs={{0,8},{4,12},{8,0},{12,4},{1,9},{5,13},{9,1},{13,5},{2,10},{6,14},... | collective-permute-start | bytes 245768 | tf_op jit(solution)/shard_map/ppermute | solution.py:388
  16.3 1.5 %collective-permute-start.2 = (bf16[2,8,2560]{2,1,0:T(8,128)(2,1)S(1)}, bf16[2,8,2560]{2,1,0:T(8,128)(2,1)S(1)}, u32[]{:S(2)}, u32[]{:S(2)}) collective-permute-start(bf16[2,8,2560]{2,1,0:T(8,128)(2,1)S(1)} %get-tuple-element.12), channel_id=1, source_target_pairs={{0,12},{4,0},{8,4},{12,8},{1,13},{5,1},{9,5},{13,9},{2,14},{6,2},{... | collective-permute-start | bytes 245768 | tf_op jit(solution)/shard_map/ppermute | solution.py:388
  17.7 3.5 %collective-permute-done.rest_1_ = bf16[2,8,2560]{2,1,0:T(8,128)(2,1)S(1)} collective-permute-done((bf16[2,8,2560]{2,1,0:T(8,128)(2,1)S(1)}, bf16[2,8,2560]{2,1,0:T(8,128)(2,1)S(1)}, u32[]{:S(2)}, u32[]{:S(2)}) %collective-permute-start) | collective-permute-done | bytes 81952 | tf_op jit(solution)/shard_map/ppermute | solution.py:388
  21.2 3.2 %collective-permute-done.1.rest_2_ = bf16[2,8,2560]{2,1,0:T(8,128)(2,1)S(1)} collective-permute-done((bf16[2,8,2560]{2,1,0:T(8,128)(2,1)S(1)}, bf16[2,8,2560]{2,1,0:T(8,128)(2,1)S(1)}, u32[]{:S(2)}, u32[]{:S(2)}) %collective-permute-start.1) | collective-permute-done | bytes 81952 | tf_op jit(solution)/shard_map/ppermute | solution.py:388
  24.5 0.0 collective-permute-done.2.rest_3_
  24.5 2.3 %attention.1 = bf16[8,8,2048]{2,1,0:T(8,128)(2,1)} custom-call(s32[6,9]{1,0:T(8,128)S(1)} %get-tuple-element.9.plan, bf16[256,256]{1,0:T(8,128)(2,1)S(1)} %copy-done.2, bf16[256,256]{1,0:T(8,128)(2,1)S(1)} %copy-done.3, f32[80,128]{1,0:T(8,128)S(1)} %copy-done.1, f32[80,128]{1,0:T(8,128)S(1)} %copy-done, bf16[2,8,2560]{2,1,0:T(8,128)(2,1)S(1)} %get-tuple-element.8._.rest_0_, ...), custom_call_target="tpu_custom_call" | custom-call | flops 100000000 | bytes 15000000 | tf_op jit(solution)/shard_map/attention/pallas_call | solution.py:413
  26.8 0.0 all-to-all-done
  26.8 1.4 %place_pages.1 = bf16[16,2,1024]{2,1,0:T(2,128)(2,1)} custom-call(s32[6,9]{1,0:T(8,128)S(1)} %get-tuple-element.9.plan, bf16[4,4,16,256]{3,2,1,0:T(8,128)(2,1)S(1)} %bitcast.6), custom_call_target="tpu_custom_call" | custom-call | flops 1000000 | bytes 5000000 | tf_op jit(solution)/shard_map/place_pages/pallas_call | solution.py:424
  (12 shorter events, 0.0 us)
Async XLA Ops:
  0.6 1.2 %copy-start = (f32[80,128]{1,0:T(8,128)S(1)}, f32[80,128]{1,0:T(8,128)}, u32[]{:S(2)}) copy-start(f32[80,128]{1,0:T(8,128)} %constant.5.clone.sine) | copy-start | bytes 122884
  0.6 1.2 %copy-start.1 = (f32[80,128]{1,0:T(8,128)S(1)}, f32[80,128]{1,0:T(8,128)}, u32[]{:S(2)}) copy-start(f32[80,128]{1,0:T(8,128)} %constant.4.clone.cosine) | copy-start | bytes 122884
  0.7 1.2 %copy-start.4 = (bf16[64,256]{1,0:T(8,128)(2,1)S(1)}, bf16[64,256]{1,0:T(8,128)(2,1)}, u32[]{:S(2)}) copy-start(bf16[64,256]{1,0:T(8,128)(2,1)} %param.14) | copy-start | bytes 98308
  0.7 1.2 %copy-start.5 = (bf16[64,256]{1,0:T(8,128)(2,1)S(1)}, bf16[64,256]{1,0:T(8,128)(2,1)}, u32[]{:S(2)}) copy-start(bf16[64,256]{1,0:T(8,128)(2,1)} %param.15) | copy-start | bytes 98308
  0.7 1.2 %copy-start.6 = (s32[4,4]{1,0:T(4,128)S(1)}, s32[4,4]{1,0:T(4,128)}, u32[]{:S(2)}) copy-start(s32[4,4]{1,0:T(4,128)} %new_blocks.1) | copy-start | bytes 196
  0.7 1.2 %copy-start.7 = (s32[4,4]{1,0:T(4,128)S(1)}, s32[4,4]{1,0:T(4,128)}, u32[]{:S(2)}) copy-start(s32[4,4]{1,0:T(4,128)} %prefix_len.1) | copy-start | bytes 196
  0.7 1.2 %copy-start.8 = (s32[4,4]{1,0:T(4,128)S(1)}, s32[4,4]{1,0:T(4,128)}, u32[]{:S(2)}) copy-start(s32[4,4]{1,0:T(4,128)} %owner.1) | copy-start | bytes 196
  0.7 1.2 %copy-start.9 = (s32[4,4]{1,0:T(4,128)S(1)}, s32[4,4]{1,0:T(4,128)}, u32[]{:S(2)}) copy-start(s32[4,4]{1,0:T(4,128)} %page_start.1) | copy-start | bytes 196
  1.8 0.7 %copy-start.10 = (s32[4]{0:T(128)S(1)}, s32[4]{0:T(128)}, u32[]{:S(2)}) copy-start(s32[4]{0:T(128)} %spread.1) | copy-start | bytes 52
  1.8 0.7 %copy-start.11 = (s32[4]{0:T(128)S(1)}, s32[4]{0:T(128)}, u32[]{:S(2)}) copy-start(s32[4]{0:T(128)} %turn.1) | copy-start | bytes 52
  4.4 20.0 %copy-start.2 = (bf16[256,256]{1,0:T(8,128)(2,1)S(1)}, bf16[256,256]{1,0:T(8,128)(2,1)}, u32[]{:S(2)}) copy-start(bf16[256,256]{1,0:T(8,128)(2,1)} %prefix_keys.1) | copy-start | bytes 393220
  4.5 20.0 %copy-start.3 = (bf16[256,256]{1,0:T(8,128)(2,1)S(1)}, bf16[256,256]{1,0:T(8,128)(2,1)}, u32[]{:S(2)}) copy-start(bf16[256,256]{1,0:T(8,128)(2,1)} %prefix_values.1) | copy-start | bytes 393220
  4.5 22.4 %all-to-all-start = ((bf16[16,16,256]{2,1,0:T(8,128)(2,1)}), bf16[16,16,256]{2,1,0:T(8,128)(2,1)S(1)}, u32[]{:S(2)}, u32[]{:S(2)}) async-start(bf16[16,16,256]{2,1,0:T(8,128)(2,1)} %get-tuple-element.13), calls=%async_computation | async-start | bytes 262144 | tf_op jit(solution)/shard_map/all_to_all | solution.py:411
  12.0 9.3 %collective-permute-start = (bf16[2,8,2560]{2,1,0:T(8,128)(2,1)S(1)}, bf16[2,8,2560]{2,1,0:T(8,128)(2,1)S(1)}, u32[]{:S(2)}, u32[]{:S(2)}) collective-permute-start(bf16[2,8,2560]{2,1,0:T(8,128)(2,1)S(1)} %get-tuple-element.10), channel_id=1, source_target_pairs={{0,4},{4,8},{8,12},{12,0},{1,5},{5,9},{9,13},{13,1},{2,6},{6,10},{... | collective-permute-start | bytes 245768 | tf_op jit(solution)/shard_map/ppermute | solution.py:388
  13.9 10.6 %collective-permute-start.1 = (bf16[2,8,2560]{2,1,0:T(8,128)(2,1)S(1)}, bf16[2,8,2560]{2,1,0:T(8,128)(2,1)S(1)}, u32[]{:S(2)}, u32[]{:S(2)}) collective-permute-start(bf16[2,8,2560]{2,1,0:T(8,128)(2,1)S(1)} %get-tuple-element.11), channel_id=1, source_target_pairs={{0,8},{4,12},{8,0},{12,4},{1,9},{5,13},{9,1},{13,5},{2,10},{6,14},... | collective-permute-start | bytes 245768 | tf_op jit(solution)/shard_map/ppermute | solution.py:388
  16.3 8.2 %collective-permute-start.2 = (bf16[2,8,2560]{2,1,0:T(8,128)(2,1)S(1)}, bf16[2,8,2560]{2,1,0:T(8,128)(2,1)S(1)}, u32[]{:S(2)}, u32[]{:S(2)}) collective-permute-start(bf16[2,8,2560]{2,1,0:T(8,128)(2,1)S(1)} %get-tuple-element.12), channel_id=1, source_target_pairs={{0,12},{4,0},{8,4},{12,8},{1,13},{5,1},{9,5},{13,9},{2,14},{6,2},{... | collective-permute-start | bytes 245768 | tf_op jit(solution)/shard_map/ppermute | solution.py:388
where the time goes:
time: 28.5 us; the launch traced here: 28.2 us
  starting transfers between devices  13.3 us (47%)
  Pallas kernels  6.78 us (24%)
  waiting for transfers between devices  6.75 us (24%)
  between operations  0.82 us (3%)
  local copies, waits for them, and re-layouts  0.63 us (2%)
    all_to_all x1, starting transfers between devices, per_device(): lax.all_to_all(finished, ('group', 'tensor'), split_axis=0, concat_axis=0...  7.5 us
    ppermute x3, waiting for transfers between devices, per_device(): lax.ppermute(sent[d], 'group', [(g, (g + d) % groups) for g in range(grou...  6.75 us
    ppermute x3, starting transfers between devices, per_device(): lax.ppermute(sent[d], 'group', [(g, (g + d) % groups) for g in range(grou...  5.75 us
    pallas_call x1, Pallas kernels, per_device(): pl.pallas_call(functools.partial(attention_kernel, groups, heads_q, heads...  2.33 us
    pallas_call x1, Pallas kernels, per_device(): pl.pallas_call(functools.partial(pages_kernel, groups, tensors), out_shap...  1.96 us
    pallas_call x1, Pallas kernels, per_device(): pl.pallas_call(functools.partial(cache_kernel, groups, tensors), out_shap...  1.42 us
    pallas_call x1, Pallas kernels, per_device(): pl.pallas_call(functools.partial(dispatch_kernel, groups), out_shape=[chu...  1.07 us
    unnamed x24, local copies, waits for them, and re-layouts  0.63 us
  transfers between devices with their start and end apart: 4, of which 2 were waited for; matrix products, arithmetic and copies ran while one was open for 0% of the time, Pallas kernels for 8%

commit v1 on v0

--- a/solution.py
+++ b/solution.py
@@ -403,7 +403,7 @@
             pltpu.SMEM((slots,), jnp.int32),
             pltpu.SMEM((slots,), jnp.int32),
         ],
-        cost_estimate=pl.CostEstimate(flops=10**7, bytes_accessed=6 * 10**6, transcendentals=0),
+        cost_estimate=pl.CostEstimate(flops=10**7, bytes_accessed=60 * 10**6, transcendentals=0),
         name="finish_pages",
     )(
         spread, turn, new_blocks, prefix_len, owner, page_start, blocks_k, blocks_v, cosine, sine, sent[0]
@@ -417,7 +417,7 @@
         out_specs=VMEM,
         scratch_shapes=[pltpu.VMEM((slots, BLOCK, width_k), jnp.float32)] * 2,
         compiler_params=params,
-        cost_estimate=pl.CostEstimate(flops=10**8, bytes_accessed=15 * 10**6, transcendentals=0),
+        cost_estimate=pl.CostEstimate(flops=10**8, bytes_accessed=200 * 10**6, transcendentals=0),
         name="attention",
     )(plan, prefix_keys, prefix_values, cosine, sine, *arrived)
 

time: 28.5 us -> 28.5 us (level)
  no operation moved by 1% of the time
where the time goes in v1:
time: 28.5 us; the launch traced here: 28.2 us
  starting transfers between devices  13.3 us (47%)
  Pallas kernels  6.78 us (24%)
  waiting for transfers between devices  6.75 us (24%)
  between operations  0.82 us (3%)
  local copies, waits for them, and re-layouts  0.63 us (2%)
    all_to_all x1, starting transfers between devices, per_device(): lax.all_to_all(finished, ('group', 'tensor'), split_axis=0, concat_axis=0...  7.5 us
    ppermute x3, waiting for transfers between devices, per_device(): lax.ppermute(sent[d], 'group', [(g, (g + d) % groups) for g in range(grou...  6.75 us
    ppermute x3, starting transfers between devices, per_device(): lax.ppermute(sent[d], 'group', [(g, (g + d) % groups) for g in range(grou...  5.75 us
    pallas_call x1, Pallas kernels, per_device(): pl.pallas_call(functools.partial(attention_kernel, groups, heads_q, heads...  2.33 us
    pallas_call x1, Pallas kernels, per_device(): pl.pallas_call(functools.partial(pages_kernel, groups, tensors), out_shap...  1.96 us
    pallas_call x1, Pallas kernels, per_device(): pl.pallas_call(functools.partial(cache_kernel, groups, tensors), out_shap...  1.42 us
    pallas_call x1, Pallas kernels, per_device(): pl.pallas_call(functools.partial(dispatch_kernel, groups), out_shape=[chu...  1.07 us
    unnamed x24, local copies, waits for them, and re-layouts  0.63 us
  transfers between devices with their start and end apart: 4, of which 2 were waited for; matrix products, arithmetic and copies ran while one was open for 0% of the time, Pallas kernels for 8%

profile of v1, /device:TPU:0, one launch (start us, length us, event | category | flops | bytes accessed | tf_op | source)
XLA Modules:
  0.0 28.2 jit_solution(13679779736742583764)
XLA Ops:
  0.6 0.0 copy-start
  0.6 0.0 copy-start.1
  0.7 1.1 %dispatch.1 = (bf16[2,8,2560]{2,1,0:T(8,128)(2,1)S(1)}, bf16[2,8,2560]{2,1,0:T(8,128)(2,1)S(1)}, bf16[2,8,2560]{2,1,0:T(8,128)(2,1)S(1)}, bf16[2,8,2560]{2,1,0:T(8,128)(2,1)S(1)}) custom-call(s32[4]{0:T(128)} %spread.1, s32[4]{0:T(128)} %turn.1, bf16[8,8,2048]{2,1,0:T(8,128)(2,1)} %bitcast.12, bf16[8,8,256]{2,1,0:T(8,128)(2,1)} %bitcast.7, ...), custom_call_target="tpu_custom_call" | custom-call | flops 1000000 | bytes 5000000 | tf_op jit(solution)/shard_map/dispatch/pallas_call | solution.py:370
  1.8 0.0 copy-start.10
  1.8 0.0 copy-start.11
  1.8 0.0 copy-done
  1.8 0.0 copy-done.1
  1.8 0.0 copy-done.4
  1.9 0.0 copy-done.5
  1.9 0.6 %copy-done.10 = s32[4]{0:T(128)S(1)} copy-done((s32[4]{0:T(128)S(1)}, s32[4]{0:T(128)}, u32[]{:S(2)}) %copy-start.10) | copy-done | bytes 40
  2.5 0.0 copy-done.11
  2.5 2.0 %finish_pages.1 = (bf16[16,16,256]{2,1,0:T(8,128)(2,1)}, s32[6,9]{1,0:T(8,128)S(1)}) custom-call(s32[4]{0:T(128)S(1)} %copy-done.10, s32[4]{0:T(128)S(1)} %copy-done.11, s32[4,4]{1,0:T(4,128)S(1)} %copy-done.6, s32[4,4]{1,0:T(4,128)S(1)} %copy-done.7, s32[4,4]{1,0:T(4,128)S(1)} %copy-done.8, s32[4,4]{1,0:T(4,128)S(1)} %copy-done.9, ...), custom_call_target="tpu_custom_call" | custom-call | flops 10000000 | bytes 60000000 | tf_op jit(solution)/shard_map/finish_pages/pallas_call | solution.py:392
  4.4 0.0 copy-start.2
  4.5 0.0 copy-start.3
  4.5 7.5 %all-to-all-start = ((bf16[16,16,256]{2,1,0:T(8,128)(2,1)}), bf16[16,16,256]{2,1,0:T(8,128)(2,1)S(1)}, u32[]{:S(2)}, u32[]{:S(2)}) async-start(bf16[16,16,256]{2,1,0:T(8,128)(2,1)} %get-tuple-element.13), calls=%async_computation | async-start | bytes 262144 | tf_op jit(solution)/shard_map/all_to_all | solution.py:411
  12.0 1.9 %collective-permute-start = (bf16[2,8,2560]{2,1,0:T(8,128)(2,1)S(1)}, bf16[2,8,2560]{2,1,0:T(8,128)(2,1)S(1)}, u32[]{:S(2)}, u32[]{:S(2)}) collective-permute-start(bf16[2,8,2560]{2,1,0:T(8,128)(2,1)S(1)} %get-tuple-element.10), channel_id=1, source_target_pairs={{0,4},{4,8},{8,12},{12,0},{1,5},{5,9},{9,13},{13,1},{2,6},{6,10},{... | collective-permute-start | bytes 245768 | tf_op jit(solution)/shard_map/ppermute | solution.py:388
  13.9 2.4 %collective-permute-start.1 = (bf16[2,8,2560]{2,1,0:T(8,128)(2,1)S(1)}, bf16[2,8,2560]{2,1,0:T(8,128)(2,1)S(1)}, u32[]{:S(2)}, u32[]{:S(2)}) collective-permute-start(bf16[2,8,2560]{2,1,0:T(8,128)(2,1)S(1)} %get-tuple-element.11), channel_id=1, source_target_pairs={{0,8},{4,12},{8,0},{12,4},{1,9},{5,13},{9,1},{13,5},{2,10},{6,14},... | collective-permute-start | bytes 245768 | tf_op jit(solution)/shard_map/ppermute | solution.py:388
  16.3 1.5 %collective-permute-start.2 = (bf16[2,8,2560]{2,1,0:T(8,128)(2,1)S(1)}, bf16[2,8,2560]{2,1,0:T(8,128)(2,1)S(1)}, u32[]{:S(2)}, u32[]{:S(2)}) collective-permute-start(bf16[2,8,2560]{2,1,0:T(8,128)(2,1)S(1)} %get-tuple-element.12), channel_id=1, source_target_pairs={{0,12},{4,0},{8,4},{12,8},{1,13},{5,1},{9,5},{13,9},{2,14},{6,2},{... | collective-permute-start | bytes 245768 | tf_op jit(solution)/shard_map/ppermute | solution.py:388
  17.7 3.5 %collective-permute-done.rest_1_ = bf16[2,8,2560]{2,1,0:T(8,128)(2,1)S(1)} collective-permute-done((bf16[2,8,2560]{2,1,0:T(8,128)(2,1)S(1)}, bf16[2,8,2560]{2,1,0:T(8,128)(2,1)S(1)}, u32[]{:S(2)}, u32[]{:S(2)}) %collective-permute-start) | collective-permute-done | bytes 81952 | tf_op jit(solution)/shard_map/ppermute | solution.py:388
  21.2 3.2 %collective-permute-done.1.rest_2_ = bf16[2,8,2560]{2,1,0:T(8,128)(2,1)S(1)} collective-permute-done((bf16[2,8,2560]{2,1,0:T(8,128)(2,1)S(1)}, bf16[2,8,2560]{2,1,0:T(8,128)(2,1)S(1)}, u32[]{:S(2)}, u32[]{:S(2)}) %collective-permute-start.1) | collective-permute-done | bytes 81952 | tf_op jit(solution)/shard_map/ppermute | solution.py:388
  24.5 0.0 collective-permute-done.2.rest_3_
  24.5 2.3 %attention.1 = bf16[8,8,2048]{2,1,0:T(8,128)(2,1)} custom-call(s32[6,9]{1,0:T(8,128)S(1)} %get-tuple-element.9.plan, bf16[256,256]{1,0:T(8,128)(2,1)S(1)} %copy-done.2, bf16[256,256]{1,0:T(8,128)(2,1)S(1)} %copy-done.3, f32[80,128]{1,0:T(8,128)S(1)} %copy-done.1, f32[80,128]{1,0:T(8,128)S(1)} %copy-done, bf16[2,8,2560]{2,1,0:T(8,128)(2,1)S(1)} %get-tuple-element.8._.rest_0_, ...), custom_call_target="tpu_custom_call" | custom-call | flops 100000000 | bytes 200000000 | tf_op jit(solution)/shard_map/attention/pallas_call | solution.py:413
  26.8 0.0 all-to-all-done
  26.8 1.4 %place_pages.1 = bf16[16,2,1024]{2,1,0:T(2,128)(2,1)} custom-call(s32[6,9]{1,0:T(8,128)S(1)} %get-tuple-element.9.plan, bf16[4,4,16,256]{3,2,1,0:T(8,128)(2,1)S(1)} %bitcast.6), custom_call_target="tpu_custom_call" | custom-call | flops 1000000 | bytes 5000000 | tf_op jit(solution)/shard_map/place_pages/pallas_call | solution.py:424
  (12 shorter events, 0.0 us)
Async XLA Ops:
  0.6 1.2 %copy-start = (f32[80,128]{1,0:T(8,128)S(1)}, f32[80,128]{1,0:T(8,128)}, u32[]{:S(2)}) copy-start(f32[80,128]{1,0:T(8,128)} %constant.5.clone.sine) | copy-start | bytes 122884
  0.6 1.2 %copy-start.1 = (f32[80,128]{1,0:T(8,128)S(1)}, f32[80,128]{1,0:T(8,128)}, u32[]{:S(2)}) copy-start(f32[80,128]{1,0:T(8,128)} %constant.4.clone.cosine) | copy-start | bytes 122884
  0.7 1.2 %copy-start.4 = (bf16[64,256]{1,0:T(8,128)(2,1)S(1)}, bf16[64,256]{1,0:T(8,128)(2,1)}, u32[]{:S(2)}) copy-start(bf16[64,256]{1,0:T(8,128)(2,1)} %param.14) | copy-start | bytes 98308
  0.7 1.2 %copy-start.5 = (bf16[64,256]{1,0:T(8,128)(2,1)S(1)}, bf16[64,256]{1,0:T(8,128)(2,1)}, u32[]{:S(2)}) copy-start(bf16[64,256]{1,0:T(8,128)(2,1)} %param.15) | copy-start | bytes 98308
  0.7 1.2 %copy-start.6 = (s32[4,4]{1,0:T(4,128)S(1)}, s32[4,4]{1,0:T(4,128)}, u32[]{:S(2)}) copy-start(s32[4,4]{1,0:T(4,128)} %new_blocks.1) | copy-start | bytes 196
  0.7 1.2 %copy-start.7 = (s32[4,4]{1,0:T(4,128)S(1)}, s32[4,4]{1,0:T(4,128)}, u32[]{:S(2)}) copy-start(s32[4,4]{1,0:T(4,128)} %prefix_len.1) | copy-start | bytes 196
  0.7 1.2 %copy-start.8 = (s32[4,4]{1,0:T(4,128)S(1)}, s32[4,4]{1,0:T(4,128)}, u32[]{:S(2)}) copy-start(s32[4,4]{1,0:T(4,128)} %owner.1) | copy-start | bytes 196
  0.7 1.2 %copy-start.9 = (s32[4,4]{1,0:T(4,128)S(1)}, s32[4,4]{1,0:T(4,128)}, u32[]{:S(2)}) copy-start(s32[4,4]{1,0:T(4,128)} %page_start.1) | copy-start | bytes 196
  1.8 0.7 %copy-start.10 = (s32[4]{0:T(128)S(1)}, s32[4]{0:T(128)}, u32[]{:S(2)}) copy-start(s32[4]{0:T(128)} %spread.1) | copy-start | bytes 52
  1.8 0.7 %copy-start.11 = (s32[4]{0:T(128)S(1)}, s32[4]{0:T(128)}, u32[]{:S(2)}) copy-start(s32[4]{0:T(128)} %turn.1) | copy-start | bytes 52
  4.4 20.0 %copy-start.2 = (bf16[256,256]{1,0:T(8,128)(2,1)S(1)}, bf16[256,256]{1,0:T(8,128)(2,1)}, u32[]{:S(2)}) copy-start(bf16[256,256]{1,0:T(8,128)(2,1)} %prefix_keys.1) | copy-start | bytes 393220
  4.5 20.0 %copy-start.3 = (bf16[256,256]{1,0:T(8,128)(2,1)S(1)}, bf16[256,256]{1,0:T(8,128)(2,1)}, u32[]{:S(2)}) copy-start(bf16[256,256]{1,0:T(8,128)(2,1)} %prefix_values.1) | copy-start | bytes 393220
  4.5 22.4 %all-to-all-start = ((bf16[16,16,256]{2,1,0:T(8,128)(2,1)}), bf16[16,16,256]{2,1,0:T(8,128)(2,1)S(1)}, u32[]{:S(2)}, u32[]{:S(2)}) async-start(bf16[16,16,256]{2,1,0:T(8,128)(2,1)} %get-tuple-element.13), calls=%async_computation | async-start | bytes 262144 | tf_op jit(solution)/shard_map/all_to_all | solution.py:411
  12.0 9.3 %collective-permute-start = (bf16[2,8,2560]{2,1,0:T(8,128)(2,1)S(1)}, bf16[2,8,2560]{2,1,0:T(8,128)(2,1)S(1)}, u32[]{:S(2)}, u32[]{:S(2)}) collective-permute-start(bf16[2,8,2560]{2,1,0:T(8,128)(2,1)S(1)} %get-tuple-element.10), channel_id=1, source_target_pairs={{0,4},{4,8},{8,12},{12,0},{1,5},{5,9},{9,13},{13,1},{2,6},{6,10},{... | collective-permute-start | bytes 245768 | tf_op jit(solution)/shard_map/ppermute | solution.py:388
  13.9 10.6 %collective-permute-start.1 = (bf16[2,8,2560]{2,1,0:T(8,128)(2,1)S(1)}, bf16[2,8,2560]{2,1,0:T(8,128)(2,1)S(1)}, u32[]{:S(2)}, u32[]{:S(2)}) collective-permute-start(bf16[2,8,2560]{2,1,0:T(8,128)(2,1)S(1)} %get-tuple-element.11), channel_id=1, source_target_pairs={{0,8},{4,12},{8,0},{12,4},{1,9},{5,13},{9,1},{13,5},{2,10},{6,14},... | collective-permute-start | bytes 245768 | tf_op jit(solution)/shard_map/ppermute | solution.py:388
  16.3 8.2 %collective-permute-start.2 = (bf16[2,8,2560]{2,1,0:T(8,128)(2,1)S(1)}, bf16[2,8,2560]{2,1,0:T(8,128)(2,1)S(1)}, u32[]{:S(2)}, u32[]{:S(2)}) collective-permute-start(bf16[2,8,2560]{2,1,0:T(8,128)(2,1)S(1)} %get-tuple-element.12), channel_id=1, source_target_pairs={{0,12},{4,0},{8,4},{12,8},{1,13},{5,1},{9,5},{13,9},{2,14},{6,2},{... | collective-permute-start | bytes 245768 | tf_op jit(solution)/shard_map/ppermute | solution.py:388
